TPU v7x, 256 devices: a whole 4x4x8 slice. The times are simulated.
256 devices in a mesh: ocn: 8 (over z), atm: 32 (over y, x, core).
Axes of the slice: x: 4, y: 4, z: 8, core: 2. Of those that a mesh axis runs over, the one named last changes fastest.
Arguments:
- atm_fields: bfloat16 [2048, 32, 128], P('atm'), may hold values from -6 to 6
- weights: bfloat16 [98304, 128, 128], P(('ocn', 'atm')), may hold values from -0.5 to 0.5
- surf_temp: float32 [98304, 128], P(('ocn', 'atm')), may hold values from -6 to 6
- surf_hum: float32 [98304, 128], P(('ocn', 'atm')), may hold values from -6 to 6
- roughness: float32 [98304, 128], P(('ocn', 'atm')), may hold values from 0.0001 to 0.1
- cell_area: float32 [98304, 128], P(('ocn', 'atm')), may hold values from 0.2 to 2
- need_list: int32 [256, 32, 4], P(('ocn', 'atm')), may hold values from 0 to 63
- use_slot: int32 [98304], P(('ocn', 'atm')), may hold values from 0 to 127, as said below
- ocean_block: int32 [98304], P(('ocn', 'atm')), may hold values from 0 to 31
- ocean_cell: int32 [98304, 128], P(('ocn', 'atm')), may hold values from 0 to 127
- cell_count: int32 [98304], P(('ocn', 'atm')), may hold values from 1 to 128, as said below
- ice_mask: int32 [98304, 128], P(('ocn', 'atm')), may hold values 0 or 1
Outputs:
- atm_flux: float32 [2048, 4, 128], P('atm')
- ocean_flux: float32 [256, 32, 128], P(('ocn', 'atm'))
Inputs may be any that keep to these rules, and one draw needn't show every extreme that they name: `use_slot`: within the 384 exchange blocks of each device every slot value appears at least once. `cell_count`: each device has a block with 128 live cells and one with a single live cell.
All inputs are finite; a program needn't handle non-finite values. No bound on the sum of `ice_mask` on one device may be relied on, other than what follows from the above.
Results may differ from a plain program's by a relative error of at most 0.00087.
Values may be sent and summed in bfloat16 or wider, within the bound.
No kernel may reach another device: no remote copies, remote signals or barrier semaphores. Data moves between devices by JAX's collectives and lax.ppermute only.
A program may use at most 128 MiB of HBM per device.

v0:
```python
import math
import jax
import jax.numpy as jnp
from jax import lax
from jax.sharding import PartitionSpec as P

F = 32
BLK = 128
ACELL = 128
OCELL = 128
CAP = 4
ITERS = 8
OBD = 1
ref_height = 10.0
karman = 0.4
buoyancy = 0.5
flux_scale = 40.0


def similarity(wind_speed, temp_diff, hum_diff, log_mom, log_heat, psi_mom, psi_heat):
    fric_vel = karman * wind_speed / (log_mom - psi_mom)
    temp_scale = karman * temp_diff / (log_heat - psi_heat)
    hum_scale = karman * hum_diff / (log_heat - psi_heat)
    return (fric_vel, temp_scale, hum_scale)


def bulk_fluxes(mapped, surf_temp, surf_hum, roughness, ice_frac):
    wind_u = 6.0 * mapped[:, 0]
    wind_v = 6.0 * mapped[:, 1]
    wind_speed = jnp.sqrt(wind_u * wind_u + wind_v * wind_v + 1.0)
    temp_diff = mapped[:, 2] - surf_temp
    hum_diff = (mapped[:, 3] - surf_hum) * (1.0 - 0.6 * ice_frac)
    log_mom = jnp.log(ref_height / roughness)
    log_heat = log_mom + math.log(10.0)
    psi_mom = jnp.zeros_like(wind_speed)
    psi_heat = jnp.zeros_like(wind_speed)
    for sweep in range(ITERS):
        fric_vel, temp_scale, hum_scale = similarity(
            wind_speed, temp_diff, hum_diff, log_mom, log_heat, psi_mom, psi_heat
        )
        stability = jnp.clip(
            ref_height * karman * buoyancy * (temp_scale + 0.2 * hum_scale) / (fric_vel * fric_vel),
            -5.0,
            1.0,
        )
        unstable = jnp.minimum(stability, 0.0)
        root_term = jnp.sqrt(jnp.sqrt(1.0 - 16.0 * unstable))
        square_term = jnp.log((1.0 + root_term * root_term) / 2.0)
        psi_mom = jnp.where(
            stability >= 0.0,
            -5.0 * stability,
            2.0 * jnp.log((1.0 + root_term) / 2.0)
            + square_term
            - 2.0 * jnp.arctan(root_term)
            + math.pi / 2.0,
        )
        psi_heat = jnp.where(stability >= 0.0, -5.0 * stability, 2.0 * square_term)
    fric_vel, temp_scale, hum_scale = similarity(
        wind_speed, temp_diff, hum_diff, log_mom, log_heat, psi_mom, psi_heat
    )
    return jnp.stack(
        [
            flux_scale * fric_vel * fric_vel * wind_u / wind_speed,
            flux_scale * fric_vel * fric_vel * wind_v / wind_speed,
            -flux_scale * fric_vel * temp_scale,
            -flux_scale * fric_vel * hum_scale,
        ],
        axis=1,
    )


def per_device(
    atm_fields,
    weights,
    surf_temp,
    surf_hum,
    roughness,
    cell_area,
    need_list,
    use_slot,
    ocean_block,
    ocean_cell,
    cell_count,
    ice_mask,
):
    owners = lax.axis_size("atm")
    local_blocks = atm_fields.shape[0]
    slot_total = owners * CAP
    block_total = weights.shape[0]
    wanted = need_list[0]
    requests = lax.all_to_all(wanted, "atm", split_axis=0, concat_axis=0, tiled=True)
    served = atm_fields[requests.reshape(-1)].reshape(owners, CAP, F, ACELL)
    arrived = lax.all_to_all(served, "atm", split_axis=0, concat_axis=0, tiled=True)
    table = arrived.reshape(slot_total, F, ACELL)
    picked = table[use_slot]
    mapped = jnp.einsum("kfa,kba->kfb", picked, weights, preferred_element_type=jnp.float32)
    ice_frac = ice_mask.astype(jnp.float32)
    flux4 = bulk_fluxes(mapped, surf_temp, surf_hum, roughness, ice_frac)
    is_live = (jnp.arange(BLK, dtype=jnp.int32)[None, :] < cell_count[:, None]).astype(jnp.float32)
    cell_weight = cell_area * is_live
    weighted = (cell_weight[:, None, :] * flux4).astype(jnp.bfloat16)
    contrib = jnp.einsum("kcb,kba->kca", weighted, weights, preferred_element_type=jnp.float32)
    slot_hot = (use_slot[:, None] == jnp.arange(slot_total, dtype=jnp.int32)[None, :]).astype(
        jnp.float32
    )
    slot_sums = jnp.dot(
        slot_hot.T, contrib.reshape(block_total, 4 * ACELL), precision=lax.Precision.HIGHEST
    )
    returned = lax.all_to_all(
        slot_sums.reshape(owners, CAP, 4 * ACELL), "atm", split_axis=0, concat_axis=0, tiled=True
    )
    owner_hot = (
        requests.reshape(-1)[:, None] == jnp.arange(local_blocks, dtype=jnp.int32)[None, :]
    ).astype(jnp.float32)
    owner_sums = jnp.dot(
        owner_hot.T, returned.reshape(slot_total, 4 * ACELL), precision=lax.Precision.HIGHEST
    )
    atm_flux = lax.psum(owner_sums, "ocn").reshape(local_blocks, 4, ACELL)
    passive = mapped[:, 4:] * (1.0 - 0.7 * ice_frac)[:, None, :]
    ocean_values = cell_weight[:, None, :] * jnp.concatenate([flux4, passive], axis=1)
    cell_hot = (ocean_cell[:, :, None] == jnp.arange(OCELL, dtype=jnp.int32)[None, None, :]).astype(
        jnp.float32
    )
    partial_sum = jnp.einsum(
        "kfb,kbc->kfc", ocean_values, cell_hot, precision=lax.Precision.HIGHEST
    )
    flat_partial = partial_sum.reshape(block_total, F * OCELL)
    targets = jnp.arange(lax.axis_size("atm") * OBD, dtype=jnp.int32)
    picker = (ocean_block[None, :] == targets[:, None]).astype(jnp.float32)
    ocean_rows = lax.psum_scatter(
        jnp.dot(picker, flat_partial, precision=lax.Precision.HIGHEST),
        "atm",
        scatter_dimension=0,
        tiled=True,
    )
    ocean_flux = ocean_rows.reshape(OBD, F, OCELL)
    return (atm_flux, ocean_flux)


def solution(mesh):
    placed = (
        P("atm", None, None),
        P(("ocn", "atm"), None, None),
        P(("ocn", "atm"), None),
        P(("ocn", "atm"), None),
        P(("ocn", "atm"), None),
        P(("ocn", "atm"), None),
        P(("ocn", "atm"), None, None),
        P(("ocn", "atm")),
        P(("ocn", "atm")),
        P(("ocn", "atm"), None),
        P(("ocn", "atm")),
        P(("ocn", "atm"), None),
    )
    return jax.shard_map(
        per_device,
        mesh=mesh,
        in_specs=placed,
        out_specs=(P("atm", None, None), P(("ocn", "atm"), None, None)),
        check_vma=False,
    )
```

profile of v0, /device:TPU:2, one launch (start us, length us, event | category | flops | bytes accessed | tf_op | source)
XLA Modules:
  0.0 347.1 jit_solution(1982289157801807212)
XLA Ops:
  7.2 0.8 copy.35
  8.0 13.6 %all_to_all.19 = s32[32,1,4]{2,1,0:T(1,128)S(1)} all-to-all(s32[32,1,4]{2,1,0:T(1,128)S(1)} %copy.35), channel_id=1, replica_groups=mesh['ocn'=8,'atm'=32] {'atm'}, dimensions={0} | all-to-all | bytes 1024 | tf_op jit(solution)/shard_map/all_to_all | solution.py:91
  21.6 0.1 reshape.90
  21.7 1.7 gather_fusion
  23.4 5.0 %all-to-all-start.1 = ((bf16[32,4,32,128]{3,2,1,0:T(8,128)(2,1)}), bf16[32,4,32,128]{3,2,1,0:T(8,128)(2,1)S(1)}, u32[]{:S(2)}, u32[]{:S(2)}) async-start(bf16[32,4,32,128]{3,2,1,0:T(8,128)(2,1)} %bitcast.2), calls=%async_computation.1 | async-start | bytes 2097152 | tf_op jit(solution)/shard_map/all_to_all | solution.py:93
  28.4 0.7 compare_select_fusion
  29.1 1.0 fusion.16
  30.2 14.5 %all-to-all-done.1 = bf16[32,4,32,128]{3,2,1,0:T(8,128)(2,1)S(1)} async-done(((bf16[32,4,32,128]{3,2,1,0:T(8,128)(2,1)}), bf16[32,4,32,128]{3,2,1,0:T(8,128)(2,1)S(1)}, u32[]{:S(2)}, u32[]{:S(2)}) %all-to-all-start.1) | async-done | bytes 1048608 | tf_op jit(solution)/shard_map/all_to_all | solution.py:93
  44.6 3.2 gather_fusion.1
  47.9 14.9 %fusion.27 = f32[384,32,128]{2,1,0:T(8,128)} fusion(bf16[384,32,128]{2,1,0:T(8,128)(2,1)} %gather_fusion.1, bf16[384,128,128]{2,1,0:T(8,128)(2,1)} %param.13), kind=kOutput, calls=%fused_computation.64 | convolution fusion | flops 402653184 | bytes 22020096 | tf_op jit(solution)/shard_map/kfa,kba->kfb/dot_general | solution.py:96
  62.8 4.0 %fusion.26 = (f32[384,1,128]{2,1,0:T(1,128)S(1)}, f32[384,1,128]{2,1,0:T(1,128)S(1)}, f32[384,1,128]{2,1,0:T(1,128)S(1)}, f32[384,1,128]{2,1,0:T(1,128)S(1)}) fusion(f32[384,32,128]{2,1,0:T(8,128)} %fusion.27), kind=kLoop, calls=%fused_computation.63 | loop fusion | bytes 1572864 | tf_op jit(solution)/shard_map/slice | solution.py:31
  66.8 5.4 %fusion.15 = (f32[384,128]{1,0:T(8,128)S(1)}, f32[384,128]{1,0:T(8,128)S(1)}, f32[384,128]{1,0:T(8,128)S(1)}) fusion(f32[384,1,128]{2,0,1:T(8,128)S(1)} %bitcast.87, f32[384,1,128]{2,0,1:T(8,128)S(1)} %bitcast.85, f32[384,128]{1,0:T(8,128)S(1)} %copy-done.2, s32[384,128]{1,0:T(8,128)S(1)} %copy-done.3, f32[384,128]{1,0:T(8,128)S(1)} %bitcast.89, ...), kind=kLoop, calls=%fused_computation.24 | loop fusion | flops 12337152 | bytes 2162688 | tf_op jit(solution)/shard_map/div | solution.py:63
  72.2 0.4 divide_multiply_fusion.1
  72.6 3.6 %slice_multiply_fusion = f32[384,28,128]{2,1,0:T(8,128)} fusion(f32[384,32,128]{2,1,0:T(8,128)S(1)} %copy-done.1, f32[384,128]{1,0:T(8,128)S(1)} %get-tuple-element.11), kind=kLoop, calls=%fused_computation.8 | loop fusion | flops 1376256 | bytes 11206656 | tf_op jit(solution)/shard_map/mul | solution.py:119
  76.3 30.8 %concatenate.4 = f32[384,32,128]{2,1,0:T(8,128)} concatenate(f32[384,1,128]{2,1,0:T(1,128)S(1)} %bitcast.81, f32[384,1,128]{2,1,0:T(1,128)S(1)} %bitcast.79, f32[384,1,128]{2,1,0:T(1,128)S(1)} %bitcast.75, f32[384,1,128]{2,1,0:T(1,128)S(1)} %bitcast.77, f32[384,28,128]{2,1,0:T(8,128)} %slice_multiply_fusion), dimensions={1} | concatenate | bytes 12582912 | tf_op jit(solution)/shard_map/concatenate | solution.py:120
  107.1 6.4 %fusion.8 = f32[384,4,128]{2,1,0:T(4,128)S(1)} fusion(bf16[384,128,128]{2,1,0:T(8,128)(2,1)} %param.13, f32[384,1,128]{2,1,0:T(1,128)S(1)} %bitcast.78, f32[384,1,128]{2,1,0:T(1,128)S(1)} %bitcast.76, f32[384,1,128]{2,1,0:T(1,128)S(1)} %bitcast.80, f32[384,1,128]{2,1,0:T(1,128)S(1)} %bitcast.82, f32[384,128]{1,0:T(8,128)S(1)} %fusion.16), kind=kOutput, calls=%fused_computation.13 | convolution fusion | flops 51314688 | bytes 14352384 | tf_op jit(solution)/shard_map/kcb,kba->kca/dot_general | solution.py:102
  113.4 0.3 reshape.115
  113.8 0.5 fusion.17
  114.3 0.9 copy.42
  115.1 5.2 %all-to-all-start.2 = ((f32[32,4,512]{2,1,0:T(4,128)}), f32[32,4,512]{2,1,0:T(4,128)S(1)}, u32[]{:S(2)}, u32[]{:S(2)}) async-start(f32[32,4,512]{2,1,0:T(4,128)} %copy.42), calls=%async_computation.2 | async-start | bytes 524288 | tf_op jit(solution)/shard_map/all_to_all | solution.py:109
  120.4 20.6 %fusion = f32[384,32,128]{2,1,0:T(8,128)S(1)} fusion(s32[384,128]{1,0:T(8,128)S(1)} %copy-done.6, f32[384,32,128]{2,1,0:T(8,128)} %concatenate.4, f32[384,128]{1,0:T(8,128)S(1)} %fusion.16), kind=kOutput, calls=%fused_computation.3 | convolution fusion | flops 2423783424 | bytes 12976128 | tf_op jit(solution)/shard_map/kfb,kbc->kfc/dot_general | solution.py:124
  141.0 6.6 %fusion.2 = f32[32,4096]{1,0:T(8,128)} fusion(f32[48,8,32,128]{3,2,1,0:T(8,128)S(1)} %bitcast.73, s32[384]{0:T(512)S(1)} %copy-done.8), kind=kOutput, calls=%fused_computation.5 | convolution fusion | flops 603992064 | bytes 6817280 | tf_op jit(solution)/shard_map/dot_general | solution.py:131
  147.7 0.6 dynamic-slice
  148.4 0.5 broadcast.204
  148.9 0.7 reduce.5
  149.6 0.1 eq.72
  149.8 0.3 fusion.21
  150.1 0.7 reshape.95
  150.8 112.9 %all-reduce.6.cloned.1.call-done = f32[32,4096]{1,0:T(8,128)} async-done(((f32[32,4096]{1,0:T(8,128)}), f32[32,4096]{1,0:T(8,128)}) %all-reduce.6.cloned.1.call-update) | async-done | bytes 524304
  263.7 2.2 constant_dynamic-slice_fusion
  265.9 72.8 %all-reduce.4.cloned.1.call-done = f32[64,4,128]{2,1,0:T(4,128)} async-done(((f32[64,4,128]{2,1,0:T(4,128)}), f32[64,4,128]{2,1,0:T(4,128)}) %all-reduce.4.cloned.1.call-update) | async-done | bytes 131088 | tf_op jit(solution)/shard_map/psum | solution.py:118
  338.7 1.6 copy.56
  (30 shorter events, 0.3 us)
Async XLA Ops:
  7.2 14.5 %copy-start = (bf16[64,32,128]{2,1,0:T(8,128)(2,1)S(1)}, bf16[64,32,128]{2,1,0:T(8,128)(2,1)}, u32[]{:S(2)}) copy-start(bf16[64,32,128]{2,1,0:T(8,128)(2,1)} %param.12) | copy-start | bytes 1572868
  23.4 21.3 %all-to-all-start.1 = ((bf16[32,4,32,128]{3,2,1,0:T(8,128)(2,1)}), bf16[32,4,32,128]{3,2,1,0:T(8,128)(2,1)S(1)}, u32[]{:S(2)}, u32[]{:S(2)}) async-start(bf16[32,4,32,128]{3,2,1,0:T(8,128)(2,1)} %bitcast.2), calls=%async_computation.1 | async-start | bytes 2097152 | tf_op jit(solution)/shard_map/all_to_all | solution.py:93
  47.8 18.9 %copy-start.2 = (f32[384,128]{1,0:T(8,128)S(1)}, f32[384,128]{1,0:T(8,128)}, u32[]{:S(2)}) copy-start(f32[384,128]{1,0:T(8,128)} %param.16) | copy-start | bytes 589828
  47.8 18.9 %copy-start.3 = (s32[384,128]{1,0:T(8,128)S(1)}, s32[384,128]{1,0:T(8,128)}, u32[]{:S(2)}) copy-start(s32[384,128]{1,0:T(8,128)} %param.23) | copy-start | bytes 589828
  47.9 18.9 %copy-start.4 = (f32[384,128]{1,0:T(8,128)S(1)}, f32[384,128]{1,0:T(8,128)}, u32[]{:S(2)}) copy-start(f32[384,128]{1,0:T(8,128)} %param.15) | copy-start | bytes 589828
  47.9 18.9 %copy-start.5 = (f32[384,128]{1,0:T(8,128)S(1)}, f32[384,128]{1,0:T(8,128)}, u32[]{:S(2)}) copy-start(f32[384,128]{1,0:T(8,128)} %param.14) | copy-start | bytes 589828
  62.8 9.9 %copy-start.1 = (f32[384,32,128]{2,1,0:T(8,128)S(1)}, f32[384,32,128]{2,1,0:T(8,128)}, u32[]{:S(2)}) copy-start(f32[384,32,128]{2,1,0:T(8,128)} %fusion.27) | copy-start | bytes 18874372
  107.0 6.7 %copy-start.7 = (s32[384]{0:T(512)S(1)}, s32[384]{0:T(512)}, u32[]{:S(2)}) copy-start(s32[384]{0:T(512)} %param.19) | copy-start | bytes 4612
  107.1 13.3 %copy-start.6 = (s32[384,128]{1,0:T(8,128)S(1)}, s32[384,128]{1,0:T(8,128)}, u32[]{:S(2)}) copy-start(s32[384,128]{1,0:T(8,128)} %param.21) | copy-start | bytes 589828
  115.1 34.5 %all-to-all-start.2 = ((f32[32,4,512]{2,1,0:T(4,128)}), f32[32,4,512]{2,1,0:T(4,128)S(1)}, u32[]{:S(2)}, u32[]{:S(2)}) async-start(f32[32,4,512]{2,1,0:T(4,128)} %copy.42), calls=%async_computation.2 | async-start | bytes 524288 | tf_op jit(solution)/shard_map/all_to_all | solution.py:109
  120.3 20.7 %copy-start.8 = (s32[384]{0:T(512)S(1)}, s32[384]{0:T(512)}, u32[]{:S(2)}) copy-start(s32[384]{0:T(512)} %param.20) | copy-start | bytes 4612
  120.3 143.4 %all-reduce.6.cloned.1.call-start = ((), (), s32[]{:S(2)}) async-start(), calls=%async_computation.4 | async-start | bytes 1048576
  141.0 6.7 %copy-start.9 = (u32[256]{0:T(256)S(1)}, u32[256]{0:T(256)}, u32[]{:S(2)}) copy-start(u32[256]{0:T(256)} %constant.72) | copy-start | bytes 3076
  147.7 191.1 %all-reduce.4.cloned.1.call-start = ((), (), s32[]{:S(2)}) async-start(), calls=%async_computation.3 | async-start | bytes 262144 | tf_op jit(solution)/shard_map/psum | solution.py:118
Sparse Core Ops, SparseCore 0:
  147.8 115.9 all-reduce.5
  266.7 71.9 all-reduce.3
where the time goes:
time: 348 us; the launch traced here: 347 us
  waiting for transfers between devices  200 us (57%)
  matrix products  49.3 us (14%)
  local copies, waits for them, and re-layouts  47.6 us (14%)
  between operations  14.3 us (4%)
  blocking collectives  13.6 us (4%)
  other arithmetic  11.9 us (3%)
  starting transfers between devices  10.3 us (3%)
    unnamed x3, waiting for transfers between devices  113 us
    psum x1, waiting for transfers between devices, per_device(): atm_flux = lax.psum(owner_sums, 'ocn').reshape(local_blocks, 4, ACELL)  72.8 us
    concatenate x1, local copies, waits for them, and re-layouts, per_device(): jnp.concatenate([flux4, passive], axis=1)  30.8 us
    dot_general x1, matrix products, per_device(): jnp.einsum('kfb,kbc->kfc', ocean_values, cell_hot, precision=lax.Precisio...  20.6 us
    dot_general x1, matrix products, per_device(): jnp.einsum('kfa,kba->kfb', picked, weights, preferred_element_type=jnp.fl...  14.9 us
    all_to_all x1, waiting for transfers between devices, per_device(): lax.all_to_all(served, 'atm', split_axis=0, concat_axis=0, tiled=True)  14.5 us
    all_to_all x1, blocking collectives, per_device(): lax.all_to_all(wanted, 'atm', split_axis=0, concat_axis=0, tiled=True)  13.6 us
  transfers between devices with their start and end apart: 4, of which 3 were waited for; matrix products, arithmetic and copies ran while one was open for 10% of the time, Pallas kernels for 0%

commit v1 on v0

--- a/solution.py
+++ b/solution.py
@@ -115,7 +115,7 @@
     owner_sums = jnp.dot(
         owner_hot.T, returned.reshape(slot_total, 4 * ACELL), precision=lax.Precision.HIGHEST
     )
-    atm_flux = lax.psum(owner_sums, "ocn").reshape(local_blocks, 4, ACELL)
+    atm_flux = jnp.sum(lax.all_gather(owner_sums, "ocn"), axis=0).reshape(local_blocks, 4, ACELL)
     passive = mapped[:, 4:] * (1.0 - 0.7 * ice_frac)[:, None, :]
     ocean_values = cell_weight[:, None, :] * jnp.concatenate([flux4, passive], axis=1)
     cell_hot = (ocean_cell[:, :, None] == jnp.arange(OCELL, dtype=jnp.int32)[None, None, :]).astype(

time: 348 us -> 279 us (0.80)
  waiting for transfers between devices: 200 us -> 128 us
    psum x1 -> x0, waiting for transfers between devices: 72.8 us -> none  [per_device(): atm_flux = lax.psum(owner_sums, 'ocn').reshape(local_blocks, 4, ACELL)]
  transfers between devices with their start and end apart: 4 -> 4, of which waited for: 3 -> 2; matrix products, arithmetic and copies ran while one was open for 10% -> 12% of each run, Pallas kernels for 0% -> 0%
where the time goes in v1:
time: 279 us; the launch traced here: 276 us
  waiting for transfers between devices  128 us (46%)
  matrix products  49.9 us (18%)
  local copies, waits for them, and re-layouts  46 us (16%)
  between operations  15.7 us (6%)
  blocking collectives  13.6 us (5%)
  other arithmetic  13.2 us (5%)
  starting transfers between devices  10.3 us (4%)
    unnamed x3, waiting for transfers between devices  113 us
    concatenate x1, local copies, waits for them, and re-layouts, per_device(): jnp.concatenate([flux4, passive], axis=1)  30.8 us
    dot_general x1, matrix products, per_device(): jnp.einsum('kfb,kbc->kfc', ocean_values, cell_hot, precision=lax.Precisio...  20.6 us
    dot_general x1, matrix products, per_device(): jnp.einsum('kfa,kba->kfb', picked, weights, preferred_element_type=jnp.fl...  14.9 us
    all_to_all x1, waiting for transfers between devices, per_device(): lax.all_to_all(served, 'atm', split_axis=0, concat_axis=0, tiled=True)  14.5 us
    all_to_all x1, blocking collectives, per_device(): lax.all_to_all(wanted, 'atm', split_axis=0, concat_axis=0, tiled=True)  13.6 us
    dot_general x1, matrix products, per_device(): jnp.dot(picker, flat_partial, precision=lax.Precision.HIGHEST)  6.61 us
    dot_general x1, matrix products, per_device(): jnp.einsum('kcb,kba->kca', weighted, weights, preferred_element_type=jnp....  6.39 us
  transfers between devices with their start and end apart: 4, of which 2 were waited for; matrix products, arithmetic and copies ran while one was open for 12% of the time, Pallas kernels for 0%

profile of v1, /device:TPU:2, one launch (start us, length us, event | category | flops | bytes accessed | tf_op | source)
XLA Modules:
  0.0 276.4 jit_solution(17777410647694757156)
XLA Ops:
  8.0 0.8 copy.35
  8.8 13.6 %all_to_all.19 = s32[32,1,4]{2,1,0:T(1,128)S(1)} all-to-all(s32[32,1,4]{2,1,0:T(1,128)S(1)} %copy.35), channel_id=1, replica_groups=mesh['ocn'=8,'atm'=32] {'atm'}, dimensions={0} | all-to-all | bytes 1024 | tf_op jit(solution)/shard_map/all_to_all | solution.py:91
  22.4 0.1 reshape.90
  22.5 1.7 gather_fusion
  24.2 5.0 %all-to-all-start.1 = ((bf16[32,4,32,128]{3,2,1,0:T(8,128)(2,1)}), bf16[32,4,32,128]{3,2,1,0:T(8,128)(2,1)S(1)}, u32[]{:S(2)}, u32[]{:S(2)}) async-start(bf16[32,4,32,128]{3,2,1,0:T(8,128)(2,1)} %bitcast.2), calls=%async_computation.1 | async-start | bytes 2097152 | tf_op jit(solution)/shard_map/all_to_all | solution.py:93
  29.2 0.7 compare_select_fusion
  29.9 1.0 fusion.16
  31.0 14.5 %all-to-all-done.1 = bf16[32,4,32,128]{3,2,1,0:T(8,128)(2,1)S(1)} async-done(((bf16[32,4,32,128]{3,2,1,0:T(8,128)(2,1)}), bf16[32,4,32,128]{3,2,1,0:T(8,128)(2,1)S(1)}, u32[]{:S(2)}, u32[]{:S(2)}) %all-to-all-start.1) | async-done | bytes 1048608 | tf_op jit(solution)/shard_map/all_to_all | solution.py:93
  45.5 3.2 %gather_fusion.1 = bf16[384,32,128]{2,1,0:T(8,128)(2,1)} fusion(bf16[128,32,128]{2,1,0:T(8,128)(2,1)S(1)} %bitcast.75, s32[1024]{0:T(1024)S(1)} %pad_clamp_fusion), kind=kCustom, calls=%fused_computation.1 | custom fusion | bytes 6292992 | tf_op jit(solution)/shard_map/gather | solution.py:95
  48.7 14.9 %fusion.27 = f32[384,32,128]{2,1,0:T(8,128)} fusion(bf16[384,32,128]{2,1,0:T(8,128)(2,1)} %gather_fusion.1, bf16[384,128,128]{2,1,0:T(8,128)(2,1)} %param.13), kind=kOutput, calls=%fused_computation.64 | convolution fusion | flops 402653184 | bytes 22020096 | tf_op jit(solution)/shard_map/kfa,kba->kfb/dot_general | solution.py:96
  63.6 4.0 %fusion.26 = (f32[384,1,128]{2,1,0:T(1,128)S(1)}, f32[384,1,128]{2,1,0:T(1,128)S(1)}, f32[384,1,128]{2,1,0:T(1,128)S(1)}, f32[384,1,128]{2,1,0:T(1,128)S(1)}) fusion(f32[384,32,128]{2,1,0:T(8,128)} %fusion.27), kind=kLoop, calls=%fused_computation.63 | loop fusion | bytes 1572864 | tf_op jit(solution)/shard_map/slice | solution.py:31
  67.6 5.4 %fusion.15 = (f32[384,128]{1,0:T(8,128)S(1)}, f32[384,128]{1,0:T(8,128)S(1)}, f32[384,128]{1,0:T(8,128)S(1)}) fusion(f32[384,1,128]{2,0,1:T(8,128)S(1)} %bitcast.89, f32[384,1,128]{2,0,1:T(8,128)S(1)} %bitcast.87, f32[384,128]{1,0:T(8,128)S(1)} %copy-done.2, s32[384,128]{1,0:T(8,128)S(1)} %copy-done.3, f32[384,128]{1,0:T(8,128)S(1)} %bitcast.91, ...), kind=kLoop, calls=%fused_computation.24 | loop fusion | flops 12337152 | bytes 2162688 | tf_op jit(solution)/shard_map/div | solution.py:63
  73.0 0.4 divide_multiply_fusion.1
  73.5 3.6 %slice_multiply_fusion = f32[384,28,128]{2,1,0:T(8,128)} fusion(f32[384,32,128]{2,1,0:T(8,128)S(1)} %copy-done.1, f32[384,128]{1,0:T(8,128)S(1)} %get-tuple-element.11), kind=kLoop, calls=%fused_computation.8 | loop fusion | flops 1376256 | bytes 11206656 | tf_op jit(solution)/shard_map/mul | solution.py:119
  77.1 30.8 %concatenate.4 = f32[384,32,128]{2,1,0:T(8,128)} concatenate(f32[384,1,128]{2,1,0:T(1,128)S(1)} %bitcast.83, f32[384,1,128]{2,1,0:T(1,128)S(1)} %bitcast.80, f32[384,1,128]{2,1,0:T(1,128)S(1)} %bitcast.76, f32[384,1,128]{2,1,0:T(1,128)S(1)} %bitcast.78, f32[384,28,128]{2,1,0:T(8,128)} %slice_multiply_fusion), dimensions={1} | concatenate | bytes 12582912 | tf_op jit(solution)/shard_map/concatenate | solution.py:120
  107.9 6.4 %fusion.8 = f32[384,4,128]{2,1,0:T(4,128)S(1)} fusion(bf16[384,128,128]{2,1,0:T(8,128)(2,1)} %param.13, f32[384,1,128]{2,1,0:T(1,128)S(1)} %bitcast.79, f32[384,1,128]{2,1,0:T(1,128)S(1)} %bitcast.77, f32[384,1,128]{2,1,0:T(1,128)S(1)} %bitcast.81, f32[384,1,128]{2,1,0:T(1,128)S(1)} %bitcast.84, f32[384,128]{1,0:T(8,128)S(1)} %fusion.16), kind=kOutput, calls=%fused_computation.13 | convolution fusion | flops 51314688 | bytes 14352384 | tf_op jit(solution)/shard_map/kcb,kba->kca/dot_general | solution.py:102
  114.3 0.3 reshape.116
  114.6 0.5 fusion.17
  115.1 0.9 copy.42
  116.0 5.2 %all-to-all-start.2 = ((f32[32,4,512]{2,1,0:T(4,128)}), f32[32,4,512]{2,1,0:T(4,128)S(1)}, u32[]{:S(2)}, u32[]{:S(2)}) async-start(f32[32,4,512]{2,1,0:T(4,128)} %copy.42), calls=%async_computation.2 | async-start | bytes 524288 | tf_op jit(solution)/shard_map/all_to_all | solution.py:109
  121.2 20.6 %fusion = f32[384,32,128]{2,1,0:T(8,128)S(1)} fusion(s32[384,128]{1,0:T(8,128)S(1)} %copy-done.6, f32[384,32,128]{2,1,0:T(8,128)} %concatenate.4, f32[384,128]{1,0:T(8,128)S(1)} %fusion.16), kind=kOutput, calls=%fused_computation.3 | convolution fusion | flops 2423783424 | bytes 12976128 | tf_op jit(solution)/shard_map/kfb,kbc->kfc/dot_general | solution.py:124
  141.8 6.6 %fusion.2 = f32[32,4096]{1,0:T(8,128)} fusion(f32[48,8,32,128]{3,2,1,0:T(8,128)S(1)} %bitcast.74, s32[384]{0:T(512)S(1)} %copy-done.8), kind=kOutput, calls=%fused_computation.5 | convolution fusion | flops 603992064 | bytes 6817280 | tf_op jit(solution)/shard_map/dot_general | solution.py:131
  148.5 0.5 broadcast.204
  149.0 0.7 reduce.5
  149.7 0.1 eq.72
  149.9 0.1 reshape.94
  150.0 1.0 fusion.21
  151.0 0.6 dynamic-slice
  151.6 113.2 %all-reduce.3.cloned.1.call-done = f32[32,4096]{1,0:T(8,128)} async-done(((f32[32,4096]{1,0:T(8,128)}), f32[32,4096]{1,0:T(8,128)}) %all-reduce.3.cloned.1.call-update) | async-done | bytes 524304
  264.8 2.1 constant_dynamic-slice_fusion
  267.0 1.3 reduce_sum.9
  268.3 0.7 reshape.95
  (30 shorter events, 0.2 us)
Async XLA Ops:
  8.0 14.5 %copy-start = (bf16[64,32,128]{2,1,0:T(8,128)(2,1)S(1)}, bf16[64,32,128]{2,1,0:T(8,128)(2,1)}, u32[]{:S(2)}) copy-start(bf16[64,32,128]{2,1,0:T(8,128)(2,1)} %param.12) | copy-start | bytes 1572868
  24.2 21.3 %all-to-all-start.1 = ((bf16[32,4,32,128]{3,2,1,0:T(8,128)(2,1)}), bf16[32,4,32,128]{3,2,1,0:T(8,128)(2,1)S(1)}, u32[]{:S(2)}, u32[]{:S(2)}) async-start(bf16[32,4,32,128]{3,2,1,0:T(8,128)(2,1)} %bitcast.2), calls=%async_computation.1 | async-start | bytes 2097152 | tf_op jit(solution)/shard_map/all_to_all | solution.py:93
  48.7 18.9 %copy-start.2 = (f32[384,128]{1,0:T(8,128)S(1)}, f32[384,128]{1,0:T(8,128)}, u32[]{:S(2)}) copy-start(f32[384,128]{1,0:T(8,128)} %param.16) | copy-start | bytes 589828
  48.7 18.9 %copy-start.3 = (s32[384,128]{1,0:T(8,128)S(1)}, s32[384,128]{1,0:T(8,128)}, u32[]{:S(2)}) copy-start(s32[384,128]{1,0:T(8,128)} %param.23) | copy-start | bytes 589828
  48.7 18.9 %copy-start.4 = (f32[384,128]{1,0:T(8,128)S(1)}, f32[384,128]{1,0:T(8,128)}, u32[]{:S(2)}) copy-start(f32[384,128]{1,0:T(8,128)} %param.15) | copy-start | bytes 589828
  48.7 18.9 %copy-start.5 = (f32[384,128]{1,0:T(8,128)S(1)}, f32[384,128]{1,0:T(8,128)}, u32[]{:S(2)}) copy-start(f32[384,128]{1,0:T(8,128)} %param.14) | copy-start | bytes 589828
  63.6 9.9 %copy-start.1 = (f32[384,32,128]{2,1,0:T(8,128)S(1)}, f32[384,32,128]{2,1,0:T(8,128)}, u32[]{:S(2)}) copy-start(f32[384,32,128]{2,1,0:T(8,128)} %fusion.27) | copy-start | bytes 18874372
  107.9 6.7 %copy-start.7 = (s32[384]{0:T(512)S(1)}, s32[384]{0:T(512)}, u32[]{:S(2)}) copy-start(s32[384]{0:T(512)} %param.19) | copy-start | bytes 4612
  107.9 13.3 %copy-start.6 = (s32[384,128]{1,0:T(8,128)S(1)}, s32[384,128]{1,0:T(8,128)}, u32[]{:S(2)}) copy-start(s32[384,128]{1,0:T(8,128)} %param.21) | copy-start | bytes 589828
  116.0 33.9 %all-to-all-start.2 = ((f32[32,4,512]{2,1,0:T(4,128)}), f32[32,4,512]{2,1,0:T(4,128)S(1)}, u32[]{:S(2)}, u32[]{:S(2)}) async-start(f32[32,4,512]{2,1,0:T(4,128)} %copy.42), calls=%async_computation.2 | async-start | bytes 524288 | tf_op jit(solution)/shard_map/all_to_all | solution.py:109
  121.2 20.7 %copy-start.8 = (s32[384]{0:T(512)S(1)}, s32[384]{0:T(512)}, u32[]{:S(2)}) copy-start(s32[384]{0:T(512)} %param.20) | copy-start | bytes 4612
  121.2 143.7 %all-reduce.3.cloned.1.call-start = ((), (), s32[]{:S(2)}) async-start(), calls=%async_computation.4 | async-start | bytes 1048576
  141.8 9.1 %copy-start.9 = (u32[256]{0:T(256)S(1)}, u32[256]{0:T(256)}, u32[]{:S(2)}) copy-start(u32[256]{0:T(256)} %constant.73) | copy-start | bytes 3076
  148.5 118.5 %all-gather.3.cloned.1.call-start = ((), (), s32[]{:S(2)}) async-start(), calls=%async_computation.3 | async-start | bytes 1179648 | tf_op jit(solution)/shard_map/all_gather | solution.py:118
Sparse Core Ops, SparseCore 0:
  148.6 116.1 all-reduce.2
Sparse Core Ops, SparseCore 1:
  151.3 41.4 all-gather.2
